TPU v7x, 32 devices: a whole 2x2x4 slice. The times are simulated.
32 devices in a mesh: slab: 2 (over x), row: 16 (over z, y, core).
Axes of the slice: x: 2, y: 2, z: 4, core: 2. Of those that a mesh axis runs over, the one named last changes fastest.
Arguments:
- sections: float32 [8, 512, 2048], P('slab', 'row'), parts along dimension 0, may hold values from -6 to 6
- valid: int32 [10, 16, 64], P('slab', 'row'), parts along dimension 0, may hold values 0 or 1
Outputs:
- flows: float32 [10, 2, 16, 64], P('slab', None, 'row'), parts along dimension 0
- displacement: float32 [8, 2, 16, 64], P('slab', None, 'row'), parts along dimension 0
There are 2 independent parts, one for each index of `slab`. A program takes and returns all parts, laid end to end along the dimension named above; each array names one. Nothing has to cross between parts.
All inputs are finite; a program needn't handle non-finite values. No bound on the sum of `valid` on one device may be relied on, other than what follows from the above.
Results may differ from a plain program's by a relative error of at most 0.0001.
Values sent between devices are 32-bit elements; how exact they have to be, the bound alone decides.
A program may use at most 64 MiB of HBM per device.

v0:
```python
import jax
import jax.numpy as jnp
from jax import lax
from jax.sharding import PartitionSpec as P

PATCH = 64
RADIUS = 2
STEPS = 4


def with_halo(cells, sides, width):
    for axis, dim in sides:
        count = lax.axis_size(axis)
        ends = count - 1
        head = lax.slice_in_dim(cells, 0, width, axis=dim)
        tail = lax.slice_in_dim(cells, cells.shape[dim] - width, cells.shape[dim], axis=dim)
        cells = jnp.concatenate(
            [
                lax.ppermute(tail, axis, [(i, (i + 1) % count) for i in range(ends)]),
                cells,
                lax.ppermute(head, axis, [((i + 1) % count, i) for i in range(ends)]),
            ],
            axis=dim,
        )
    return cells


def pair_list(count):
    first = [(s, s + 1) for s in range(count - 1)]
    second = [(s, s + 2) for s in range(count - 2)]
    return first + second


def patch_columns(product, node_cols):
    lead = product.shape[:-1]
    halves = product.reshape(lead + (2 * node_cols, -1)).sum(-1)
    widths = [(0, 0)] * len(lead) + [(1, 1)]
    padded = jnp.pad(halves, widths)
    left = padded[..., : 2 * node_cols].reshape(lead + (node_cols, 2)).sum(-1)
    right = padded[..., 2:].reshape(lead + (node_cols, 2)).sum(-1)
    return left + right


def band_sums(fixed_rows, moving_rows, reach, width, groups):
    moving_pad = jnp.pad(moving_rows, ((0, 0), (reach, reach)))
    results = []
    for shift_x in range(-reach, reach + 1):
        product = fixed_rows * moving_pad[:, reach + shift_x : reach + shift_x + width]
        results.append(product.reshape(groups, -1, width).sum(1))
    return jnp.stack(results)


def relax_steps(moved_nodes, flow_rows, mask_rows, pairs, multiplier):
    for turn_index in range(STEPS):
        rimmed = with_halo(moved_nodes, (("row", 2),), 1)
        sideways = jnp.pad(moved_nodes, ((0, 0), (0, 0), (0, 0), (1, 1)))
        lap = (
            4.0 * moved_nodes
            - rimmed[:, :, :-2]
            - rimmed[:, :, 2:]
            - sideways[..., :-2]
            - sideways[..., 2:]
        )
        grad = 1.0 * lap
        for index, (first, second) in enumerate(pairs):
            error = mask_rows[index][None] * (
                moved_nodes[second] - moved_nodes[first] - flow_rows[index]
            )
            grad = grad.at[second].add(error).at[first].add(-error)
        moved_nodes = moved_nodes - 0.1 * grad * multiplier
    return moved_nodes


def local(sections, valid):
    count, stride, width = sections.shape
    margin = stride // 2
    reach = RADIUS
    node_cols = width // stride
    pairs = pair_list(count)
    extended = with_halo(sections, (("row", 1),), margin + reach)
    pair_corr = []
    for first, second in pairs:
        fixed_rows = extended[first, reach : reach + stride + 2 * margin]
        shift_rows = []
        for shift_y in range(-reach, reach + 1):
            moving_rows = extended[second, reach + shift_y : reach + shift_y + stride + 2 * margin]
            row_total = band_sums(fixed_rows, moving_rows, reach, width, 1)[:, 0]
            shift_rows.append(patch_columns(row_total, node_cols))
        pair_corr.append(jnp.stack(shift_rows))
    corr = jnp.stack(pair_corr)
    corr = corr / PATCH
    offsets = jnp.arange(-reach, reach + 1).astype(jnp.float32)
    weight = corr * corr + 1.0
    denom = weight.sum((1, 2))
    flow_y = (offsets[None, :, None, None] * weight).sum((1, 2)) / denom
    flow_x = (offsets[None, None, :, None] * weight).sum((1, 2)) / denom
    flows = jnp.stack([flow_y, flow_x], axis=1)[:, :, None, :]
    masks = valid.astype(jnp.float32)
    pinned = (jnp.arange(count) > 0).astype(jnp.float32)[:, None, None, None]
    moved_nodes = jnp.zeros((count, 2, 1, node_cols), jnp.float32)
    moved_nodes = relax_steps(moved_nodes, flows, masks, pairs, pinned)
    return (flows, moved_nodes)


def solution(mesh):
    return jax.shard_map(
        local,
        mesh=mesh,
        in_specs=(P("slab", "row", None), P("slab", "row", None)),
        out_specs=(P("slab", None, "row", None), P("slab", None, "row", None)),
        check_vma=False,
    )
```

profile of v0, /device:TPU:1, one launch (start us, length us, event | category | flops | bytes accessed | tf_op | source)
XLA Modules:
  0.0 189.8 jit_solution(16174900599561937582)
XLA Ops:
  0.7 4.7 %collective-permute-start.2 = (f32[4,2,1,64]{3,1,2,0:T(2,128)S(1)}, f32[4,2,1,64]{3,1,2,0:T(2,128)S(1)}, u32[]{:S(2)}, u32[]{:S(2)}) collective-permute-start(f32[4,2,1,64]{3,1,2,0:T(2,128)S(1)} %broadcast.1053), channel_id=1, source_target_pairs={{0,1},{1,2},{2,3},{3,4},{4,5},{5,6},{6,7},{7,8},{8,9},{9,10},{10,1... | collective-permute-start | bytes 6152 | tf_op jit(solution)/shard_map/ppermute | solution.py:19
  5.3 1.9 %collective-permute-start.3 = (f32[4,2,1,64]{3,1,2,0:T(2,128)S(1)}, f32[4,2,1,64]{3,1,2,0:T(2,128)S(1)}, u32[]{:S(2)}, u32[]{:S(2)}) collective-permute-start(f32[4,2,1,64]{3,1,2,0:T(2,128)S(1)} %broadcast.1053), channel_id=1, source_target_pairs={{1,0},{2,1},{3,2},{4,3},{5,4},{6,5},{7,6},{8,7},{9,8},{10,9},{11,1... | collective-permute-start | bytes 6152 | tf_op jit(solution)/shard_map/ppermute | solution.py:21
  7.3 1.5 fusion.88
  8.8 3.6 %collective-permute-start = (f32[4,18,2048]{2,1,0:T(8,128)S(1)}, f32[4,18,2048]{2,1,0:T(8,128)S(1)}, u32[]{:S(2)}, u32[]{:S(2)}) collective-permute-start(f32[4,18,2048]{2,1,0:T(8,128)S(1)} %get-tuple-element.712), channel_id=1, source_target_pairs={{0,1},{1,2},{2,3},{3,4},{4,5},{5,6},{6,7},{7,8},{8,9},{9,10},{10,1... | collective-permute-start | bytes 1769480 | tf_op jit(solution)/shard_map/ppermute | solution.py:19
  12.5 1.9 %collective-permute-start.1 = (f32[4,18,2048]{2,1,0:T(8,128)S(1)}, f32[4,18,2048]{2,1,0:T(8,128)S(1)}, u32[]{:S(2)}, u32[]{:S(2)}) collective-permute-start(f32[4,18,2048]{2,1,0:T(8,128)S(1)} %get-tuple-element.713), channel_id=1, source_target_pairs={{1,0},{2,1},{3,2},{4,3},{5,4},{6,5},{7,6},{8,7},{9,8},{10,9},{11,1... | collective-permute-start | bytes 1769480 | tf_op jit(solution)/shard_map/ppermute | solution.py:21
  16.2 13.6 %collective-permute-done = f32[4,18,2048]{2,1,0:T(8,128)S(1)} collective-permute-done((f32[4,18,2048]{2,1,0:T(8,128)S(1)}, f32[4,18,2048]{2,1,0:T(8,128)S(1)}, u32[]{:S(2)}, u32[]{:S(2)}) %collective-permute-start) | collective-permute-done | bytes 589856 | tf_op jit(solution)/shard_map/ppermute | solution.py:19
  30.1 2.6 %multiply_reduce_fusion.12 = (f32[2048]{0:T(1024)}, f32[2048]{0:T(1024)}, f32[2048]{0:T(1024)}, f32[2048]{0:T(1024)}, f32[2048]{0:T(1024)}, /*index=5*/f32[2048]...) fusion(f32[4,68,2048]{2,1,0:T(8,128)S(1)} %pad_maximum_fusion), kind=kLoop, calls=%fused_computation.93 | loop fusion | flops 1820672 | bytes 12115968 | tf_op jit(solution)/shard_map/reduce_sum | solution.py:49
  32.7 2.6 %multiply_reduce_fusion.7 = (f32[2048]{0:T(1024)}, f32[2048]{0:T(1024)}, f32[2048]{0:T(1024)}, f32[2048]{0:T(1024)}, f32[2048]{0:T(1024)}, /*index=5*/f32[2048]{...) fusion(f32[4,68,2048]{2,1,0:T(8,128)S(1)} %pad_maximum_fusion), kind=kLoop, calls=%fused_computation.88 | loop fusion | flops 4681728 | bytes 8011776 | tf_op jit(solution)/shard_map/reduce_sum | solution.py:49
  36.2 2.9 %multiply_reduce_fusion = (f32[2048]{0:T(1024)}, f32[2048]{0:T(1024)}, f32[2048]{0:T(1024)S(1)}, f32[2048]{0:T(1024)S(1)}, f32[2048]{0:T(1024)}, /*index=5*/f32[...) fusion(f32[64,2048]{1,0:T(8,128)S(1)} %get-tuple-element.676, ...), kind=kLoop, calls=%fused_computation.81 | loop fusion | flops 4161536 | bytes 3276800 | tf_op jit(solution)/shard_map/reduce_sum | solution.py:49
  49.2 4.8 %multiply_reduce_fusion.15 = (f32[2048]{0:T(1024)}, f32[2048]{0:T(1024)}, f32[2048]{0:T(1024)S(1)}, f32[2048]{0:T(1024)S(1)}, f32[2048]{0:T(1024)}, /*index=5*/f32[2048]{0:T(1024)}, f32[2048]{0:T(1024)}, f32[2048]{0:T(1024)}) fusion(f32[64,2048]{1,0:T(8,128)} %get-tuple-element.691, f32[4,68,2048]{2,1,0:T(8,128)S(1)} %pad_maximum_fusion), kind=kLoop, calls=%fused_computation.96 | loop fusion | flops 2080768 | bytes 1638400 | tf_op jit(solution)/shard_map/reduce_sum | solution.py:49
  58.4 1.5 constant_dynamic-update-slice_fusion.128
  64.9 4.6 %multiply_reduce_fusion.20 = (f32[2048]{0:T(1024)}, f32[2048]{0:T(1024)}, f32[2048]{0:T(1024)S(1)}, f32[2048]{0:T(1024)S(1)}, f32[2048]{0:T(1024)}, /*index=5*/f32[2048]{0:T(1024)}, f32[2048]{0:T(1024)}, f32[2048]{0:T(1024)}) fusion(f32[64,2048]{1,0:T(8,128)} %get-tuple-element.692, f32[4,68,2048]{2,1,0:T(8,128)S(1)} %pad_maximum_fusion), kind=kLoop, calls=%fused_computation.101 | loop fusion | flops 2080768 | bytes 1638400 | tf_op jit(solution)/shard_map/reduce_sum | solution.py:49
  75.3 1.5 constant_dynamic-update-slice_fusion.122
  80.4 6.0 %multiply_reduce_fusion.10 = (f32[2048]{0:T(1024)}, f32[2048]{0:T(1024)}, f32[2048]{0:T(1024)S(1)}, f32[2048]{0:T(1024)S(1)}, f32[2048]{0:T(1024)}, /*index=5*/f...) fusion(f32[64,2048]{1,0:T(8,128)} %get-tuple-element.690, ...), kind=kLoop, calls=%fused_computation.91 | loop fusion | flops 3121152 | bytes 2719744 | tf_op jit(solution)/shard_map/reduce_sum | solution.py:49
  90.0 1.5 constant_dynamic-update-slice_fusion.133
  96.5 6.3 %multiply_reduce_fusion.5 = (f32[2048]{0:T(1024)S(1)}, f32[2048]{0:T(1024)S(1)}, f32[2048]{0:T(1024)S(1)}, f32[2048]{0:T(1024)S(1)}, f32[2048]{0:T(1024)}, /*ind...) fusion(f32[64,2048]{1,0:T(8,128)} %get-tuple-element.685, ...), kind=kLoop, calls=%fused_computation.86 | loop fusion | flops 4161536 | bytes 3276800 | tf_op jit(solution)/shard_map/reduce_sum | solution.py:49
  104.7 4.4 %fusion.27 = (f32[2048]{0:T(1024)S(1)}, f32[2048]{0:T(1024)S(1)}, f32[2048]{0:T(1024)S(1)}, f32[2048]{0:T(1024)S(1)}, f32[2048]{0:T(1024)}, /*index=5*/f32[2048]{0:T(1024)}, f32[2048]{0:T(1024)}, f32[2048]{0:T(1024)}) fusion(f32[64,2048]{1,0:T(8,128)} %get-tuple-element.705, f32[4,68,2048]{2,1,0:T(8,128)S(1)} %pad_maximum_fusion), kind=kLoop, calls=%fused_computation.68 | loop fusion | flops 2080768 | bytes 1638400 | tf_op jit(solution)/shard_map/reduce_sum | solution.py:49
  111.3 1.5 constant_dynamic-update-slice_fusion.97
  116.4 1.8 fusion.23
  121.9 1.5 constant_dynamic-update-slice_fusion.92
  126.9 1.8 fusion.31
  132.4 1.5 constant_dynamic-update-slice_fusion.102
  137.5 1.8 fusion.35
  164.7 4.4 %collective-permute-start.4 = (f32[4,2,1,64]{3,1,2,0:T(2,128)S(1)}, f32[4,2,1,64]{3,1,2,0:T(2,128)S(1)}, u32[]{:S(2)}, u32[]{:S(2)}) collective-permute-start(f32[4,2,1,64]{3,1,2,0:T(2,128)S(1)} %multiply_subtract_fusion.3), channel_id=1, source_target_pairs={{0,1},{1,2},{2,3},{3,4},{4,5},{5,6},{6,7},{7,8},{8,9},{9,10},{10,1... | collective-permute-start | bytes 6152 | tf_op jit(solution)/shard_map/ppermute | solution.py:19
  169.0 1.9 %collective-permute-start.5 = (f32[4,2,1,64]{3,1,2,0:T(2,128)S(1)}, f32[4,2,1,64]{3,1,2,0:T(2,128)S(1)}, u32[]{:S(2)}, u32[]{:S(2)}) collective-permute-start(f32[4,2,1,64]{3,1,2,0:T(2,128)S(1)} %multiply_subtract_fusion.3), channel_id=1, source_target_pairs={{1,0},{2,1},{3,2},{4,3},{5,4},{6,5},{7,6},{8,7},{9,8},{10,9},{11,1... | collective-permute-start | bytes 6152 | tf_op jit(solution)/shard_map/ppermute | solution.py:21
  171.0 3.0 %collective-permute-done.5 = f32[4,2,1,64]{3,1,2,0:T(2,128)S(1)} collective-permute-done((f32[4,2,1,64]{3,1,2,0:T(2,128)S(1)}, f32[4,2,1,64]{3,1,2,0:T(2,128)S(1)}, u32[]{:S(2)}, u32[]{:S(2)}) %collective-permute-start.5) | collective-permute-done | bytes 2080 | tf_op jit(solution)/shard_map/ppermute | solution.py:21
  174.3 1.9 %collective-permute-start.6 = (f32[4,2,1,64]{3,1,2,0:T(2,128)S(1)}, f32[4,2,1,64]{3,1,2,0:T(2,128)S(1)}, u32[]{:S(2)}, u32[]{:S(2)}) collective-permute-start(f32[4,2,1,64]{3,1,2,0:T(2,128)S(1)} %multiply_subtract_fusion.2), channel_id=1, source_target_pairs={{0,1},{1,2},{2,3},{3,4},{4,5},{5,6},{6,7},{7,8},{8,9},{9,10},{10,1... | collective-permute-start | bytes 6152 | tf_op jit(solution)/shard_map/ppermute | solution.py:19
  176.2 2.4 %collective-permute-start.7 = (f32[4,2,1,64]{3,1,2,0:T(2,128)S(1)}, f32[4,2,1,64]{3,1,2,0:T(2,128)S(1)}, u32[]{:S(2)}, u32[]{:S(2)}) collective-permute-start(f32[4,2,1,64]{3,1,2,0:T(2,128)S(1)} %multiply_subtract_fusion.2), channel_id=1, source_target_pairs={{1,0},{2,1},{3,2},{4,3},{5,4},{6,5},{7,6},{8,7},{9,8},{10,9},{11,1... | collective-permute-start | bytes 6152 | tf_op jit(solution)/shard_map/ppermute | solution.py:21
  178.6 2.5 %collective-permute-done.7 = f32[4,2,1,64]{3,1,2,0:T(2,128)S(1)} collective-permute-done((f32[4,2,1,64]{3,1,2,0:T(2,128)S(1)}, f32[4,2,1,64]{3,1,2,0:T(2,128)S(1)}, u32[]{:S(2)}, u32[]{:S(2)}) %collective-permute-start.7) | collective-permute-done | bytes 2080 | tf_op jit(solution)/shard_map/ppermute | solution.py:21
  181.4 1.9 %collective-permute-start.8 = (f32[4,2,1,64]{3,1,2,0:T(2,128)S(1)}, f32[4,2,1,64]{3,1,2,0:T(2,128)S(1)}, u32[]{:S(2)}, u32[]{:S(2)}) collective-permute-start(f32[4,2,1,64]{3,1,2,0:T(2,128)S(1)} %multiply_subtract_fusion.1), channel_id=1, source_target_pairs={{0,1},{1,2},{2,3},{3,4},{4,5},{5,6},{6,7},{7,8},{8,9},{9,10},{10,1... | collective-permute-start | bytes 6152 | tf_op jit(solution)/shard_map/ppermute | solution.py:19
  183.4 2.4 %collective-permute-start.9 = (f32[4,2,1,64]{3,1,2,0:T(2,128)S(1)}, f32[4,2,1,64]{3,1,2,0:T(2,128)S(1)}, u32[]{:S(2)}, u32[]{:S(2)}) collective-permute-start(f32[4,2,1,64]{3,1,2,0:T(2,128)S(1)} %multiply_subtract_fusion.1), channel_id=1, source_target_pairs={{1,0},{2,1},{3,2},{4,3},{5,4},{6,5},{7,6},{8,7},{9,8},{10,9},{11,1... | collective-permute-start | bytes 6152 | tf_op jit(solution)/shard_map/ppermute | solution.py:21
  186.4 2.6 %collective-permute-done.9 = f32[4,2,1,64]{3,1,2,0:T(2,128)S(1)} collective-permute-done((f32[4,2,1,64]{3,1,2,0:T(2,128)S(1)}, f32[4,2,1,64]{3,1,2,0:T(2,128)S(1)}, u32[]{:S(2)}, u32[]{:S(2)}) %collective-permute-start.9) | collective-permute-done | bytes 2080 | tf_op jit(solution)/shard_map/ppermute | solution.py:21
  (733 shorter events, 86.5 us)
Async XLA Ops:
  0.6 29.2 %copy-start = (f32[4,32,2048]{2,1,0:T(8,128)S(1)}, f32[4,32,2048]{2,1,0:T(8,128)}, u32[]{:S(2)}) copy-start(f32[4,32,2048]{2,1,0:T(8,128)} %param.82) | copy-start | bytes 3145732
  0.6 14.3 %copy-start.92 = (s32[5,1,64]{2,1,0:T(1,128)S(1)}, s32[5,1,64]{2,1,0:T(1,128)}, u32[]{:S(2)}) copy-start(s32[5,1,64]{2,1,0:T(1,128)} %param.83) | copy-start | bytes 3844
  0.7 15.5 %collective-permute-start.2 = (f32[4,2,1,64]{3,1,2,0:T(2,128)S(1)}, f32[4,2,1,64]{3,1,2,0:T(2,128)S(1)}, u32[]{:S(2)}, u32[]{:S(2)}) collective-permute-start(f32[4,2,1,64]{3,1,2,0:T(2,128)S(1)} %broadcast.1053), channel_id=1, source_target_pairs={{0,1},{1,2},{2,3},{3,4},{4,5},{5,6},{6,7},{7,8},{8,9},{9,10},{10,1... | collective-permute-start | bytes 6152 | tf_op jit(solution)/shard_map/ppermute | solution.py:19
  5.3 10.8 %collective-permute-start.3 = (f32[4,2,1,64]{3,1,2,0:T(2,128)S(1)}, f32[4,2,1,64]{3,1,2,0:T(2,128)S(1)}, u32[]{:S(2)}, u32[]{:S(2)}) collective-permute-start(f32[4,2,1,64]{3,1,2,0:T(2,128)S(1)} %broadcast.1053), channel_id=1, source_target_pairs={{1,0},{2,1},{3,2},{4,3},{5,4},{6,5},{7,6},{8,7},{9,8},{10,9},{11,1... | collective-permute-start | bytes 6152 | tf_op jit(solution)/shard_map/ppermute | solution.py:21
  8.8 21.0 %collective-permute-start = (f32[4,18,2048]{2,1,0:T(8,128)S(1)}, f32[4,18,2048]{2,1,0:T(8,128)S(1)}, u32[]{:S(2)}, u32[]{:S(2)}) collective-permute-start(f32[4,18,2048]{2,1,0:T(8,128)S(1)} %get-tuple-element.712), channel_id=1, source_target_pairs={{0,1},{1,2},{2,3},{3,4},{4,5},{5,6},{6,7},{7,8},{8,9},{9,10},{10,1... | collective-permute-start | bytes 1769480 | tf_op jit(solution)/shard_map/ppermute | solution.py:19
  12.5 17.3 %collective-permute-start.1 = (f32[4,18,2048]{2,1,0:T(8,128)S(1)}, f32[4,18,2048]{2,1,0:T(8,128)S(1)}, u32[]{:S(2)}, u32[]{:S(2)}) collective-permute-start(f32[4,18,2048]{2,1,0:T(8,128)S(1)} %get-tuple-element.713), channel_id=1, source_target_pairs={{1,0},{2,1},{3,2},{4,3},{5,4},{6,5},{7,6},{8,7},{9,8},{10,9},{11,1... | collective-permute-start | bytes 1769480 | tf_op jit(solution)/shard_map/ppermute | solution.py:21
  79.7 8.1 %copy-start.78 = (f32[2048]{0:T(1024)S(1)}, f32[2048]{0:T(1024)}, u32[]{:S(2)}) copy-start(f32[2048]{0:T(1024)} %get-tuple-element.610) | copy-start | bytes 24580
  95.8 7.2 %copy-start.77 = (f32[2048]{0:T(1024)S(1)}, f32[2048]{0:T(1024)}, u32[]{:S(2)}) copy-start(f32[2048]{0:T(1024)} %get-tuple-element.601) | copy-start | bytes 24580
  102.8 7.0 %copy-start.76 = (f32[2048]{0:T(1024)S(1)}, f32[2048]{0:T(1024)}, u32[]{:S(2)}) copy-start(f32[2048]{0:T(1024)} %get-tuple-element.694) | copy-start | bytes 24580
  103.3 13.1 %copy-start.4 = (f32[64,2048]{1,0:T(8,128)S(1)}, f32[64,2048]{1,0:T(8,128)}, u32[]{:S(2)}) copy-start(f32[64,2048]{1,0:T(8,128)} %get-tuple-element.706) | copy-start | bytes 1572868
  111.3 15.6 %copy-start.3 = (f32[64,2048]{1,0:T(8,128)S(1)}, f32[64,2048]{1,0:T(8,128)}, u32[]{:S(2)}) copy-start(f32[64,2048]{1,0:T(8,128)} %get-tuple-element.704) | copy-start | bytes 1572868
  121.9 15.6 %copy-start.2 = (f32[64,2048]{1,0:T(8,128)S(1)}, f32[64,2048]{1,0:T(8,128)}, u32[]{:S(2)}) copy-start(f32[64,2048]{1,0:T(8,128)} %get-tuple-element.703) | copy-start | bytes 1572868
  132.4 8.8 %copy-start.1 = (f32[64,2048]{1,0:T(8,128)S(1)}, f32[64,2048]{1,0:T(8,128)}, u32[]{:S(2)}) copy-start(f32[64,2048]{1,0:T(8,128)} %get-tuple-element.702) | copy-start | bytes 1572868
  137.5 5.1 %copy-start.75 = (f32[2048]{0:T(1024)S(1)}, f32[2048]{0:T(1024)}, u32[]{:S(2)}) copy-start(f32[2048]{0:T(1024)} %get-tuple-element.604) | copy-start | bytes 24580
  141.2 3.8 %copy-start.31 = (f32[2048]{0:T(1024)S(1)}, f32[2048]{0:T(1024)}, u32[]{:S(2)}) copy-start(f32[2048]{0:T(1024)} %get-tuple-element.523) | copy-start | bytes 24580
  142.9 3.8 %copy-start.34 = (f32[2048]{0:T(1024)S(1)}, f32[2048]{0:T(1024)}, u32[]{:S(2)}) copy-start(f32[2048]{0:T(1024)} %get-tuple-element.528) | copy-start | bytes 24580
  142.9 3.9 %copy-start.72 = (f32[2048]{0:T(1024)S(1)}, f32[2048]{0:T(1024)}, u32[]{:S(2)}) copy-start(f32[2048]{0:T(1024)} %get-tuple-element.605) | copy-start | bytes 24580
  143.1 3.9 %copy-start.32 = (f32[2048]{0:T(1024)S(1)}, f32[2048]{0:T(1024)}, u32[]{:S(2)}) copy-start(f32[2048]{0:T(1024)} %get-tuple-element.530) | copy-start | bytes 24580
  144.3 3.8 %copy-start.38 = (f32[2048]{0:T(1024)S(1)}, f32[2048]{0:T(1024)}, u32[]{:S(2)}) copy-start(f32[2048]{0:T(1024)} %get-tuple-element.512) | copy-start | bytes 24580
  144.3 3.9 %copy-start.71 = (f32[2048]{0:T(1024)S(1)}, f32[2048]{0:T(1024)}, u32[]{:S(2)}) copy-start(f32[2048]{0:T(1024)} %get-tuple-element.609) | copy-start | bytes 24580
  144.5 3.8 %copy-start.37 = (f32[2048]{0:T(1024)S(1)}, f32[2048]{0:T(1024)}, u32[]{:S(2)}) copy-start(f32[2048]{0:T(1024)} %get-tuple-element.513) | copy-start | bytes 24580
  144.5 3.9 %copy-start.36 = (f32[2048]{0:T(1024)S(1)}, f32[2048]{0:T(1024)}, u32[]{:S(2)}) copy-start(f32[2048]{0:T(1024)} %get-tuple-element.514) | copy-start | bytes 24580
  145.6 3.8 %copy-start.42 = (f32[2048]{0:T(1024)S(1)}, f32[2048]{0:T(1024)}, u32[]{:S(2)}) copy-start(f32[2048]{0:T(1024)} %get-tuple-element.504) | copy-start | bytes 24580
  145.6 3.9 %copy-start.70 = (f32[2048]{0:T(1024)S(1)}, f32[2048]{0:T(1024)}, u32[]{:S(2)}) copy-start(f32[2048]{0:T(1024)} %get-tuple-element.611) | copy-start | bytes 24580
  145.8 3.8 %copy-start.41 = (f32[2048]{0:T(1024)S(1)}, f32[2048]{0:T(1024)}, u32[]{:S(2)}) copy-start(f32[2048]{0:T(1024)} %get-tuple-element.505) | copy-start | bytes 24580
  145.8 3.9 %copy-start.40 = (f32[2048]{0:T(1024)S(1)}, f32[2048]{0:T(1024)}, u32[]{:S(2)}) copy-start(f32[2048]{0:T(1024)} %get-tuple-element.506) | copy-start | bytes 24580
  164.7 6.3 %collective-permute-start.4 = (f32[4,2,1,64]{3,1,2,0:T(2,128)S(1)}, f32[4,2,1,64]{3,1,2,0:T(2,128)S(1)}, u32[]{:S(2)}, u32[]{:S(2)}) collective-permute-start(f32[4,2,1,64]{3,1,2,0:T(2,128)S(1)} %multiply_subtract_fusion.3), channel_id=1, source_target_pairs={{0,1},{1,2},{2,3},{3,4},{4,5},{5,6},{6,7},{7,8},{8,9},{9,10},{10,1... | collective-permute-start | bytes 6152 | tf_op jit(solution)/shard_map/ppermute | solution.py:19
  169.0 4.9 %collective-permute-start.5 = (f32[4,2,1,64]{3,1,2,0:T(2,128)S(1)}, f32[4,2,1,64]{3,1,2,0:T(2,128)S(1)}, u32[]{:S(2)}, u32[]{:S(2)}) collective-permute-start(f32[4,2,1,64]{3,1,2,0:T(2,128)S(1)} %multiply_subtract_fusion.3), channel_id=1, source_target_pairs={{1,0},{2,1},{3,2},{4,3},{5,4},{6,5},{7,6},{8,7},{9,8},{10,9},{11,1... | collective-permute-start | bytes 6152 | tf_op jit(solution)/shard_map/ppermute | solution.py:21
  174.3 4.3 %collective-permute-start.6 = (f32[4,2,1,64]{3,1,2,0:T(2,128)S(1)}, f32[4,2,1,64]{3,1,2,0:T(2,128)S(1)}, u32[]{:S(2)}, u32[]{:S(2)}) collective-permute-start(f32[4,2,1,64]{3,1,2,0:T(2,128)S(1)} %multiply_subtract_fusion.2), channel_id=1, source_target_pairs={{0,1},{1,2},{2,3},{3,4},{4,5},{5,6},{6,7},{7,8},{8,9},{9,10},{10,1... | collective-permute-start | bytes 6152 | tf_op jit(solution)/shard_map/ppermute | solution.py:19
  176.2 4.9 %collective-permute-start.7 = (f32[4,2,1,64]{3,1,2,0:T(2,128)S(1)}, f32[4,2,1,64]{3,1,2,0:T(2,128)S(1)}, u32[]{:S(2)}, u32[]{:S(2)}) collective-permute-start(f32[4,2,1,64]{3,1,2,0:T(2,128)S(1)} %multiply_subtract_fusion.2), channel_id=1, source_target_pairs={{1,0},{2,1},{3,2},{4,3},{5,4},{6,5},{7,6},{8,7},{9,8},{10,9},{11,1... | collective-permute-start | bytes 6152 | tf_op jit(solution)/shard_map/ppermute | solution.py:21
  181.4 4.9 %collective-permute-start.8 = (f32[4,2,1,64]{3,1,2,0:T(2,128)S(1)}, f32[4,2,1,64]{3,1,2,0:T(2,128)S(1)}, u32[]{:S(2)}, u32[]{:S(2)}) collective-permute-start(f32[4,2,1,64]{3,1,2,0:T(2,128)S(1)} %multiply_subtract_fusion.1), channel_id=1, source_target_pairs={{0,1},{1,2},{2,3},{3,4},{4,5},{5,6},{6,7},{7,8},{8,9},{9,10},{10,1... | collective-permute-start | bytes 6152 | tf_op jit(solution)/shard_map/ppermute | solution.py:19
  183.4 5.6 %collective-permute-start.9 = (f32[4,2,1,64]{3,1,2,0:T(2,128)S(1)}, f32[4,2,1,64]{3,1,2,0:T(2,128)S(1)}, u32[]{:S(2)}, u32[]{:S(2)}) collective-permute-start(f32[4,2,1,64]{3,1,2,0:T(2,128)S(1)} %multiply_subtract_fusion.1), channel_id=1, source_target_pairs={{1,0},{2,1},{3,2},{4,3},{5,4},{6,5},{7,6},{8,7},{9,8},{10,9},{11,1... | collective-permute-start | bytes 6152 | tf_op jit(solution)/shard_map/ppermute | solution.py:21
  (72 other events, 254.3 us)
where the time goes:
time: 192 us; the launch traced here: 190 us
  local copies, waits for them, and re-layouts  76.4 us (40%)
  other arithmetic  60.1 us (31%)
  starting transfers between devices  27.1 us (14%)
  waiting for transfers between devices  21.7 us (11%)
  between operations  4.59 us (2%)
    reduce_sum x12, other arithmetic, band_sums(): results.append(product.reshape(groups, -1, width).sum(1))  40.7 us
    another operation x150, local copies, waits for them, and re-layouts, band_sums(): return jnp.stack(results)  31.4 us
    unnamed x316, local copies, waits for them, and re-layouts  29 us
    ppermute x5, starting transfers between devices, with_halo(): lax.ppermute(tail, axis, [(i, (i + 1) % count) for i in range(ends)])  16.6 us
    ppermute x5, waiting for transfers between devices, with_halo(): lax.ppermute(tail, axis, [(i, (i + 1) % count) for i in range(ends)])  13.6 us
    reduce_sum x25, other arithmetic, patch_columns(): halves = product.reshape(lead + (2 * node_cols, -1)).sum(-1)  11 us
    ppermute x5, starting transfers between devices, with_halo(): lax.ppermute(head, axis, [((i + 1) % count, i) for i in range(ends)])  10.5 us
    ppermute x5, waiting for transfers between devices, with_halo(): lax.ppermute(head, axis, [((i + 1) % count, i) for i in range(ends)])  8.11 us
  transfers between devices with their start and end apart: 10, of which 4 were waited for; matrix products, arithmetic and copies ran while one was open for 2% of the time, Pallas kernels for 0%

commit v1 on v0

v1 whole, which is shorter than its diff:
```python
import functools

import jax
import jax.numpy as jnp
from jax import lax
from jax.experimental import pallas as pl
from jax.experimental.pallas import tpu as pltpu
from jax.sharding import PartitionSpec as P

PATCH = 64
RADIUS = 2
STEPS = 4
LANES = 128
SPAN = STEPS - 1
PAIRS = ((0, 1), (1, 2), (2, 3), (0, 2), (1, 3))
SHIFTS = 2 * RADIUS + 1
TERMS = len(PAIRS) * SHIFTS
BF16 = jnp.bfloat16
F32 = jnp.float32


def thirds(value):
    high = value.astype(BF16)
    rest = value - high.astype(F32)
    middle = rest.astype(BF16)
    low = (rest - middle.astype(F32)).astype(BF16)
    return high, middle, low


def exact_dot(value, ones):
    return sum(jnp.dot(part, ones, preferred_element_type=F32) for part in thirds(value))


def shifted(row, shift):
    if shift == 0:
        return row
    blocks = row.shape[0]
    lane = lax.broadcasted_iota(jnp.int32, row.shape, 1)
    block = lax.broadcasted_iota(jnp.int32, row.shape, 0)
    if shift > 0:
        other = jnp.where(block == blocks - 1, 0.0, pltpu.roll(row, blocks - 1, 0))
        return pltpu.roll(jnp.where(lane < shift, other, row), LANES - shift, 1)
    other = jnp.where(block == 0, 0.0, pltpu.roll(row, 1, 0))
    return pltpu.roll(jnp.where(lane >= LANES + shift, other, row), -shift, 1)


def kernel(
    rows_of, sections, valid, flows_out, moved_out,
    natural, image, moving, halo, halo_moving, sums, ones, reduced, arrived, notes,
    load_sem, halo_send, halo_recv, band_send, band_recv, note_send, note_recv,
):
    me = lax.axis_index("row")
    count, stride, width = natural.shape
    blocks = width // LANES
    halves = blocks // 8
    band = stride // 2
    node_cols = width // stride

    loads = [
        pltpu.make_async_copy(sections.at[s], natural.at[s], load_sem.at[s])
        for s in range(count)
    ]
    for load in loads:
        load.start()

    halo[...] = jnp.zeros(halo.shape, F32)
    arrived[...] = jnp.zeros(arrived.shape, F32)
    notes[...] = jnp.zeros(notes.shape, F32)
    barrier = pltpu.get_barrier_semaphore()
    offsets = [o for k in range(1, SPAN + 1) for o in (-k, k)]

    def inside(offset):
        return me >= -offset if offset < 0 else me < rows_of - offset

    for offset in offsets:
        @pl.when(inside(offset))
        def _():
            pl.semaphore_signal(
                barrier, inc=1, device_id={"row": me + offset},
                device_id_type=pl.DeviceIdType.MESH,
            )

    for b in range(2):
        for half in range(halves):
            sums[b, half, TERMS * SHIFTS * 8:, :] = jnp.zeros(
                (sums.shape[2] - TERMS * SHIFTS * 8, LANES), F32
            )
    for t in range(blocks):
        column = lax.broadcasted_iota(jnp.int32, (LANES, LANES), 0) + t * LANES
        lane = lax.broadcasted_iota(jnp.int32, (LANES, LANES), 1)
        node = jnp.where(lane < node_cols, lane, lane - node_cols)
        first = node * stride - stride // 2
        hit = (column >= first) & (column < first + PATCH)
        ones[t * LANES:(t + 1) * LANES, :] = jnp.where(hit, 1.0, 0.0).astype(BF16)

    for s in range(count):
        loads[s].wait()

        @pl.loop(0, stride // 8)
        def _(tile):
            base = pl.multiple_of((s * stride + tile * 8) * blocks, 8)
            top = pl.multiple_of(tile * 8, 8)
            for t in range(blocks):
                image[pl.ds(base + t, 8, stride=blocks), :] = natural[
                    s, pl.ds(top, 8), t * LANES:(t + 1) * LANES
                ]

    size = RADIUS * blocks
    signals = jnp.minimum(me, SPAN) + jnp.minimum(rows_of - 1 - me, SPAN)
    pl.semaphore_wait(barrier, signals)

    def halo_copy(side, s):
        row = 0 if side == 0 else stride - RADIUS
        start = (s * stride + row) * blocks
        return pltpu.make_async_remote_copy(
            src_ref=image.at[pl.ds(start, size)],
            dst_ref=halo.at[1 - side, s - 1],
            send_sem=halo_send.at[side, s - 1],
            recv_sem=halo_recv.at[1 - side, s - 1],
            device_id={"row": me - 1 if side == 0 else me + 1},
            device_id_type=pl.DeviceIdType.MESH,
        )

    def on_side(side):
        return pl.when(inside(-1 if side == 0 else 1))

    for side in range(2):
        @on_side(side)
        def _():
            for s in range(1, count):
                halo_copy(side, s).start()

    @pl.loop(0, stride)
    def _(row):
        for s in range(1, count):
            start = pl.multiple_of((s * stride + row) * blocks, 8)
            value = image[pl.ds(start, blocks), :]
            for x in range(SHIFTS):
                moving[x, s - 1, row] = shifted(value, x - RADIUS)

    @pl.loop(0, SHIFTS * halves)
    def _(turn):
        x = turn // halves
        half = turn % halves
        sub = pl.multiple_of(half * 8, 8)
        out = pl.multiple_of(x * (TERMS * 8), 8)
        for b in range(2):
            totals = [None] * TERMS
            for y in range(b * band, (b + 1) * band):
                fixed = [
                    image[pl.ds(pl.multiple_of((s * stride + y) * blocks + sub, 8), 8), :]
                    for s in range(count - 1)
                ]
                for v in range(SHIFTS):
                    other = y + v - RADIUS
                    if other < 0 or other >= stride:
                        continue
                    moved = [moving[x, s, other, pl.ds(sub, 8), :] for s in range(count - 1)]
                    for p, (first, second) in enumerate(PAIRS):
                        product = fixed[first] * moved[second - 1]
                        i = p * SHIFTS + v
                        totals[i] = product if totals[i] is None else totals[i] + product
            for i in range(TERMS):
                sums[b, half, pl.ds(pl.multiple_of(out + i * 8, 8), 8), :] = totals[i]

    for side in range(2):
        @on_side(side)
        def _():
            for s in range(1, count):
                pltpu.make_async_copy(
                    halo.at[side, s - 1], halo.at[side, s - 1], halo_recv.at[side, s - 1]
                ).wait()

    for side in range(2):
        @pl.loop(0, RADIUS)
        def _(row):
            for s in range(count - 1):
                value = halo[side, s, pl.ds(pl.multiple_of(row * blocks, 8), blocks), :]
                for x in range(SHIFTS):
                    halo_moving[x, side, s, row] = shifted(value, x - RADIUS)

    @pl.loop(0, SHIFTS * halves)
    def _(turn):
        x = turn // halves
        half = turn % halves
        sub = pl.multiple_of(half * 8, 8)
        out = pl.multiple_of(x * (TERMS * 8), 8)
        for b in range(2):
            totals = {}
            for y in range(b * band, (b + 1) * band):
                for v in range(SHIFTS):
                    other = y + v - RADIUS
                    if 0 <= other < stride:
                        continue
                    row = other + RADIUS if other < 0 else other - stride
                    for p, (first, second) in enumerate(PAIRS):
                        at = pl.multiple_of((first * stride + y) * blocks + sub, 8)
                        product = image[pl.ds(at, 8), :] * halo_moving[
                            x, b, second - 1, row, pl.ds(sub, 8), :
                        ]
                        i = p * SHIFTS + v
                        totals[i] = totals[i] + product if i in totals else product
            for i, total in totals.items():
                at = pl.ds(pl.multiple_of(out + i * 8, 8), 8)
                sums[b, half, at, :] = sums[b, half, at, :] + total

    def band_copy(side):
        return pltpu.make_async_remote_copy(
            src_ref=reduced.at[side],
            dst_ref=arrived.at[1 - side],
            send_sem=band_send.at[side],
            recv_sem=band_recv.at[1 - side],
            device_id={"row": me - 1 if side == 0 else me + 1},
            device_id_type=pl.DeviceIdType.MESH,
        )

    for b in range(2):
        total = jnp.zeros((LANES, LANES), F32)
        for t in range(0, blocks, 2):
            wide = jnp.concatenate(
                [sums[b, k // 8, pl.ds(k % 8, LANES, stride=8), :] for k in (t, t + 1)], axis=1
            )
            total = total + exact_dot(wide, ones[t * LANES:(t + 2) * LANES, :])
        reduced[b] = total

        @on_side(b)
        def _():
            band_copy(b).start()

    term = lax.broadcasted_iota(jnp.int32, (32, LANES), 1)
    line = lax.broadcasted_iota(jnp.int32, (32, LANES), 0)
    shift_x = sum((term >= TERMS * k).astype(jnp.int32) for k in range(1, SHIFTS))
    rest = term - TERMS * shift_x
    pair = sum((rest >= SHIFTS * k).astype(jnp.int32) for k in range(1, len(PAIRS)))
    shift_y = rest - SHIFTS * pair
    kind = (line >= 8).astype(jnp.int32) + (line >= 16).astype(jnp.int32)
    factor = jnp.where(kind == 0, 1, jnp.where(kind == 1, shift_y - RADIUS, shift_x - RADIUS))
    belongs = (pair == line - 8 * kind) & (term < TERMS * SHIFTS) & (line < 24)
    weights_of = jnp.where(belongs, factor, 0).astype(F32).astype(BF16)

    for side in range(2):
        @on_side(side)
        def _():
            pltpu.make_async_copy(
                arrived.at[side], arrived.at[side], band_recv.at[side]
            ).wait()

    corr = (reduced[0] + reduced[1] + arrived[0] + arrived[1]) * (1.0 / PATCH)
    weight = corr * corr + 1.0
    moments = sum(
        jnp.dot(weights_of, part, preferred_element_type=F32) for part in thirds(weight)
    )
    lane = lax.broadcasted_iota(jnp.int32, (8, LANES), 1)
    line = lax.broadcasted_iota(jnp.int32, (8, LANES), 0)
    npairs = len(PAIRS)
    denom = jnp.where(line < npairs, moments[0:8], 1.0)
    flow = jnp.where(lane < node_cols, moments[8:16], moments[16:24]) / denom
    mask = valid[:, 0, :].astype(F32)
    notes[SPAN, 0:8, :] = flow
    notes[SPAN, 8:8 + npairs, 0:node_cols] = mask
    notes[SPAN, 8:8 + npairs, node_cols:2 * node_cols] = mask

    def note_copy(k):
        offset = offsets[k]
        return pltpu.make_async_remote_copy(
            src_ref=notes.at[SPAN],
            dst_ref=notes.at[SPAN - offset],
            send_sem=note_send.at[k],
            recv_sem=note_recv.at[SPAN - offset],
            device_id={"row": me + offset},
            device_id_type=pl.DeviceIdType.MESH,
        )

    for k, offset in enumerate(offsets):
        @pl.when(inside(offset))
        def _():
            note_copy(k).start()

    flows_out[:, 0, 0, :] = flow[:npairs, :node_cols]
    flows_out[:, 1, 0, :] = flow[:npairs, node_cols:]

    for k, offset in enumerate(offsets):
        @pl.when(inside(offset))
        def _():
            slot = SPAN + offset
            pltpu.make_async_copy(notes.at[slot], notes.at[slot], note_recv.at[slot]).wait()

    node_row = me - SPAN + line
    keep = jnp.where((node_row >= 0) & (node_row < rows_of), 0.1, 0.0)
    at_left = (lane == 0) | (lane == node_cols)
    at_right = (lane == node_cols - 1) | (lane == 2 * node_cols - 1)
    flow_rows = [notes[:, p, :] for p in range(npairs)]
    mask_rows = [notes[:, 8 + p, :] for p in range(npairs)]
    moved = [jnp.zeros((8, LANES), F32) for _ in range(count)]
    for step in range(STEPS):
        grad = [None] * count
        for s in range(1, count):
            d = moved[s]
            left = jnp.where(at_left, 0.0, pltpu.roll(d, 1, 1))
            right = jnp.where(at_right, 0.0, pltpu.roll(d, LANES - 1, 1))
            grad[s] = 4.0 * d - pltpu.roll(d, 1, 0) - pltpu.roll(d, 7, 0) - left - right
        for p, (first, second) in enumerate(PAIRS):
            error = mask_rows[p] * (moved[second] - moved[first] - flow_rows[p])
            grad[second] = grad[second] + error
            if first > 0:
                grad[first] = grad[first] - error
        moved = [moved[0]] + [moved[s] - keep * grad[s] for s in range(1, count)]
    for s in range(count):
        moved_out[s, 0] = moved[s][SPAN:SPAN + 1, :node_cols]
        moved_out[s, 1] = moved[s][SPAN:SPAN + 1, node_cols:]

    for side in range(2):
        @on_side(side)
        def _():
            for s in range(1, count):
                halo_copy(side, s).wait_send()
            band_copy(side).wait_send()
    for k, offset in enumerate(offsets):
        @pl.when(inside(offset))
        def _():
            note_copy(k).wait_send()


def local(rows_of, sections, valid):
    count, stride, width = sections.shape
    blocks = width // LANES
    npairs = valid.shape[0]
    node_cols = width // stride
    moving = count - 1
    terms = TERMS * SHIFTS
    return pl.pallas_call(
        functools.partial(kernel, rows_of),
        out_shape=(
            jax.ShapeDtypeStruct((npairs, 2, 1, node_cols), F32),
            jax.ShapeDtypeStruct((count, 2, 1, node_cols), F32),
        ),
        in_specs=[
            pl.BlockSpec(memory_space=pl.ANY),
            pl.BlockSpec(memory_space=pltpu.VMEM),
        ],
        out_specs=(
            pl.BlockSpec(memory_space=pltpu.VMEM),
            pl.BlockSpec(memory_space=pltpu.VMEM),
        ),
        scratch_shapes=[
            pltpu.VMEM((count, stride, width), F32),
            pltpu.VMEM((count * stride * blocks, LANES), F32),
            pltpu.VMEM((SHIFTS, moving, stride, blocks, LANES), F32),
            pltpu.VMEM((2, moving, RADIUS * blocks, LANES), F32),
            pltpu.VMEM((SHIFTS, 2, moving, RADIUS, blocks, LANES), F32),
            pltpu.VMEM((2, blocks // 8, -(-terms // 8) * 64, LANES), F32),
            pltpu.VMEM((width, LANES), BF16),
            pltpu.VMEM((2, LANES, LANES), F32),
            pltpu.VMEM((2, LANES, LANES), F32),
            pltpu.VMEM((8, 16, LANES), F32),
            pltpu.SemaphoreType.DMA((count,)),
            pltpu.SemaphoreType.DMA((2, moving)),
            pltpu.SemaphoreType.DMA((2, moving)),
            pltpu.SemaphoreType.DMA((2,)),
            pltpu.SemaphoreType.DMA((2,)),
            pltpu.SemaphoreType.DMA((2 * SPAN,)),
            pltpu.SemaphoreType.DMA((2 * SPAN + 1,)),
        ],
        compiler_params=pltpu.CompilerParams(
            collective_id=0, has_side_effects=True, vmem_limit_bytes=32 * 2**20
        ),
    )(sections, valid)


def solution(mesh):
    return jax.shard_map(
        functools.partial(local, mesh.shape["row"]),
        mesh=mesh,
        in_specs=(P("slab", "row", None), P("slab", "row", None)),
        out_specs=(P("slab", None, "row", None), P("slab", None, "row", None)),
        check_vma=False,
    )
```

time: 192 us -> 20.7 us (0.11); the launches traced: 190 us -> 20.6 us
  local copies, waits for them, and re-layouts: 76.4 us -> 3.09 us
  other arithmetic: 60.1 us -> 0 us
  starting transfers between devices: 27.1 us -> 0 us
  waiting for transfers between devices: 21.7 us -> 0 us
  Pallas kernels: 0 us -> 16.8 us
  between operations: 4.59 us -> 0.65 us
    reduce_sum x88 -> x0, other arithmetic: 56.2 us -> none  [the longest x12 40.7 us: band_sums(): results.append(product.reshape(groups, -1, width).sum(1))]
    another operation x157 -> x0, local copies, waits for them, and re-layouts: 31.4 us -> none  [the longest x150 31.4 us: band_sums(): return jnp.stack(results)]
    ppermute x10 -> x0, starting transfers between devices: 27.1 us -> none  [the longest x5 16.6 us: with_halo(): lax.ppermute(tail, axis, [(i, (i + 1) % count) for i in range(ends)])]
    unnamed x316 -> x6, local copies, waits for them, and re-layouts: 29 us -> 3.09 us
    ppermute x10 -> x0, waiting for transfers between devices: 21.7 us -> none  [the longest x5 13.6 us: with_halo(): lax.ppermute(tail, axis, [(i, (i + 1) % count) for i in range(ends)])]
    pallas_call x0 -> x1, Pallas kernels: none -> 16.8 us  [local(): pl.pallas_call(functools.partial(kernel, rows_of), out_shape=(jax.ShapeDt...]
    slice x76 -> x0, local copies, waits for them, and re-layouts: 9.08 us -> none  [the longest x50 4.66 us: patch_columns(): right = padded[..., 2:].reshape(lead + (node_cols, 2)).sum(-1)]
    add x25 -> x0, local copies, waits for them, and re-layouts: 5.34 us -> none  [patch_columns(): return left + right]
  transfers between devices with their start and end apart: 10 -> 0, of which waited for: 4 -> 0; matrix products, arithmetic and copies ran while one was open for 2% -> 0% of each run, Pallas kernels for 0% -> 0%
where the time goes in v1:
time: 20.7 us; the launch traced here: 20.6 us
  Pallas kernels  16.8 us (81%)
  local copies, waits for them, and re-layouts  3.09 us (15%)
  between operations  0.65 us (3%)
    pallas_call x1, Pallas kernels, local(): pl.pallas_call(functools.partial(kernel, rows_of), out_shape=(jax.ShapeDt...  16.8 us
    unnamed x6, local copies, waits for them, and re-layouts  3.09 us

profile of v1, /device:TPU:1, one launch (start us, length us, event | category | flops | bytes accessed | tf_op | source)
XLA Modules:
  0.0 20.6 jit_solution(8867164798224943626)
XLA Ops:
  0.6 0.0 copy-start
  0.6 1.2 %copy-done = f32[4,32,2048]{2,1,0:T(8,128)S(1)} copy-done((f32[4,32,2048]{2,1,0:T(8,128)S(1)}, f32[4,32,2048]{2,1,0:T(8,128)}, u32[]{:S(2)}) %copy-start) | copy-done | bytes 1048600
  1.9 0.0 copy-start.1
  1.9 0.7 %copy-done.1 = s32[5,1,64]{2,1,0:T(1,128)S(1)} copy-done((s32[5,1,64]{2,1,0:T(1,128)S(1)}, s32[5,1,64]{2,1,0:T(1,128)}, u32[]{:S(2)}) %copy-start.1) | copy-done | bytes 1304
  2.5 16.8 %shard_map.41 = (f32[5,2,1,64]{3,2,1,0:T(1,128)S(1)}, f32[4,2,1,64]{3,2,1,0:T(1,128)S(1)}) custom-call(f32[4,32,2048]{2,1,0:T(8,128)S(1)} %copy-done, s32[5,1,64]{2,1,0:T(1,128)S(1)} %copy-done.1), custom_call_target="tpu_custom_call" | custom-call | tf_op jit(solution)/shard_map/pallas_call | solution.py:331
  19.4 0.6 %copy.6 = f32[5,2,1,64]{3,2,1,0:T(1,128)} copy(f32[5,2,1,64]{3,2,1,0:T(1,128)S(1)} %get-tuple-element.4) | data formatting | bytes 5120
  20.0 0.6 %copy.7 = f32[4,2,1,64]{3,2,1,0:T(1,128)} copy(f32[4,2,1,64]{3,2,1,0:T(1,128)S(1)} %get-tuple-element.5) | data formatting | bytes 4096
Async XLA Ops:
  0.6 1.2 %copy-start = (f32[4,32,2048]{2,1,0:T(8,128)S(1)}, f32[4,32,2048]{2,1,0:T(8,128)}, u32[]{:S(2)}) copy-start(f32[4,32,2048]{2,1,0:T(8,128)} %sections.1) | copy-start | bytes 3145732
  1.9 0.7 %copy-start.1 = (s32[5,1,64]{2,1,0:T(1,128)S(1)}, s32[5,1,64]{2,1,0:T(1,128)}, u32[]{:S(2)}) copy-start(s32[5,1,64]{2,1,0:T(1,128)} %valid.1) | copy-start | bytes 3844

commit v2 on v1

--- a/solution.py
+++ b/solution.py
@@ -28,7 +28,11 @@
 
 
 def exact_dot(value, ones):
-    return sum(jnp.dot(part, ones, preferred_element_type=F32) for part in thirds(value))
+    rows = value.shape[0]
+    parts = jnp.dot(
+        jnp.concatenate(thirds(value), axis=0), ones, preferred_element_type=F32
+    )
+    return parts[:rows] + parts[rows:2 * rows] + parts[2 * rows:]
 
 
 def shifted(row, shift):
@@ -45,9 +49,9 @@
 
 
 def kernel(
-    rows_of, sections, valid, flows_out, moved_out,
+    rows_of, sections, valid, rows_out,
     natural, image, moving, halo, halo_moving, sums, ones, reduced, arrived, notes,
-    load_sem, halo_send, halo_recv, band_send, band_recv, note_send, note_recv,
+    load_sem, halo_send, halo_recv, band_send, band_recv, note_send, note_recv, mask_in, mask_notes, mask_load, mask_send, mask_recv,
 ):
     me = lax.axis_index("row")
     count, stride, width = natural.shape
@@ -63,9 +67,13 @@
     for load in loads:
         load.start()
 
+    mask_copy_in = pltpu.make_async_copy(valid, mask_in, mask_load)
+    mask_copy_in.start()
+
     halo[...] = jnp.zeros(halo.shape, F32)
     arrived[...] = jnp.zeros(arrived.shape, F32)
     notes[...] = jnp.zeros(notes.shape, F32)
+    mask_notes[...] = jnp.zeros(mask_notes.shape, F32)
     barrier = pltpu.get_barrier_semaphore()
     offsets = [o for k in range(1, SPAN + 1) for o in (-k, k)]
 
@@ -98,10 +106,10 @@
 
         @pl.loop(0, stride // 8)
         def _(tile):
-            base = pl.multiple_of((s * stride + tile * 8) * blocks, 8)
+            base = pl.multiple_of(tile * 8 * blocks, 8)
             top = pl.multiple_of(tile * 8, 8)
             for t in range(blocks):
-                image[pl.ds(base + t, 8, stride=blocks), :] = natural[
+                image[s, pl.ds(base + t, 8, stride=blocks), :] = natural[
                     s, pl.ds(top, 8), t * LANES:(t + 1) * LANES
                 ]
 
@@ -109,14 +117,14 @@
     signals = jnp.minimum(me, SPAN) + jnp.minimum(rows_of - 1 - me, SPAN)
     pl.semaphore_wait(barrier, signals)
 
-    def halo_copy(side, s):
+    def halo_copy(side):
         row = 0 if side == 0 else stride - RADIUS
-        start = (s * stride + row) * blocks
+        start = row * blocks
         return pltpu.make_async_remote_copy(
-            src_ref=image.at[pl.ds(start, size)],
-            dst_ref=halo.at[1 - side, s - 1],
-            send_sem=halo_send.at[side, s - 1],
-            recv_sem=halo_recv.at[1 - side, s - 1],
+            src_ref=image.at[1:count, pl.ds(start, size)],
+            dst_ref=halo.at[1 - side],
+            send_sem=halo_send.at[side],
+            recv_sem=halo_recv.at[1 - side],
             device_id={"row": me - 1 if side == 0 else me + 1},
             device_id_type=pl.DeviceIdType.MESH,
         )
@@ -127,14 +135,35 @@
     for side in range(2):
         @on_side(side)
         def _():
-            for s in range(1, count):
-                halo_copy(side, s).start()
-
-    @pl.loop(0, stride)
+            halo_copy(side).start()
+
+    npairs = len(PAIRS)
+
+    def row_copy(k, rows, sends, recvs):
+        offset = offsets[k]
+        return pltpu.make_async_remote_copy(
+            src_ref=rows.at[SPAN],
+            dst_ref=rows.at[SPAN - offset],
+            send_sem=sends.at[k],
+            recv_sem=recvs.at[SPAN - offset],
+            device_id={"row": me + offset},
+            device_id_type=pl.DeviceIdType.MESH,
+        )
+
+    mask_copy_in.wait()
+    mask = mask_in[:, 0, :].astype(F32)
+    mask_notes[SPAN, 0:npairs, 0:node_cols] = mask
+    mask_notes[SPAN, 0:npairs, node_cols:2 * node_cols] = mask
+    for k, offset in enumerate(offsets):
+        @pl.when(inside(offset))
+        def _():
+            row_copy(k, mask_notes, mask_send, mask_recv).start()
+
+    @pl.loop(0, stride, unroll=8)
     def _(row):
         for s in range(1, count):
-            start = pl.multiple_of((s * stride + row) * blocks, 8)
-            value = image[pl.ds(start, blocks), :]
+            start = pl.multiple_of(row * blocks, 8)
+            value = image[s, pl.ds(start, blocks), :]
             for x in range(SHIFTS):
                 moving[x, s - 1, row] = shifted(value, x - RADIUS)
 
@@ -148,7 +177,7 @@
             totals = [None] * TERMS
             for y in range(b * band, (b + 1) * band):
                 fixed = [
-                    image[pl.ds(pl.multiple_of((s * stride + y) * blocks + sub, 8), 8), :]
+                    image[s, pl.ds(pl.multiple_of(y * blocks + sub, 8), 8), :]
                     for s in range(count - 1)
                 ]
                 for v in range(SHIFTS):
@@ -166,13 +195,10 @@
     for side in range(2):
         @on_side(side)
         def _():
-            for s in range(1, count):
-                pltpu.make_async_copy(
-                    halo.at[side, s - 1], halo.at[side, s - 1], halo_recv.at[side, s - 1]
-                ).wait()
+            pltpu.make_async_copy(halo.at[side], halo.at[side], halo_recv.at[side]).wait()
 
     for side in range(2):
-        @pl.loop(0, RADIUS)
+        @pl.loop(0, RADIUS, unroll=2)
         def _(row):
             for s in range(count - 1):
                 value = halo[side, s, pl.ds(pl.multiple_of(row * blocks, 8), blocks), :]
@@ -194,8 +220,8 @@
                         continue
                     row = other + RADIUS if other < 0 else other - stride
                     for p, (first, second) in enumerate(PAIRS):
-                        at = pl.multiple_of((first * stride + y) * blocks + sub, 8)
-                        product = image[pl.ds(at, 8), :] * halo_moving[
+                        at = pl.multiple_of(y * blocks + sub, 8)
+                        product = image[first, pl.ds(at, 8), :] * halo_moving[
                             x, b, second - 1, row, pl.ds(sub, 8), :
                         ]
                         i = p * SHIFTS + v
@@ -214,6 +240,7 @@
             device_id_type=pl.DeviceIdType.MESH,
         )
 
+    first_half = lax.broadcasted_iota(jnp.int32, (LANES // 2, LANES), 1) < node_cols
     for b in range(2):
         total = jnp.zeros((LANES, LANES), F32)
         for t in range(0, blocks, 2):
@@ -221,7 +248,7 @@
                 [sums[b, k // 8, pl.ds(k % 8, LANES, stride=8), :] for k in (t, t + 1)], axis=1
             )
             total = total + exact_dot(wide, ones[t * LANES:(t + 2) * LANES, :])
-        reduced[b] = total
+        reduced[b] = jnp.where(first_half, total[:LANES // 2], total[LANES // 2:])
 
         @on_side(b)
         def _():
@@ -247,50 +274,65 @@
 
     corr = (reduced[0] + reduced[1] + arrived[0] + arrived[1]) * (1.0 / PATCH)
     weight = corr * corr + 1.0
-    moments = sum(
-        jnp.dot(weights_of, part, preferred_element_type=F32) for part in thirds(weight)
+    parts = thirds(weight)
+    low, high = (
+        sum(jnp.dot(half, part, preferred_element_type=F32) for part in parts)
+        for half in (weights_of[:, :LANES // 2], weights_of[:, LANES // 2:])
     )
+    moments = jnp.where(
+        lax.broadcasted_iota(jnp.int32, low.shape, 1) < node_cols, low, high
+    )
+    moments = moments + pltpu.roll(moments, LANES // 2, 1)
     lane = lax.broadcasted_iota(jnp.int32, (8, LANES), 1)
     line = lax.broadcasted_iota(jnp.int32, (8, LANES), 0)
-    npairs = len(PAIRS)
     denom = jnp.where(line < npairs, moments[0:8], 1.0)
     flow = jnp.where(lane < node_cols, moments[8:16], moments[16:24]) / denom
-    mask = valid[:, 0, :].astype(F32)
-    notes[SPAN, 0:8, :] = flow
-    notes[SPAN, 8:8 + npairs, 0:node_cols] = mask
-    notes[SPAN, 8:8 + npairs, node_cols:2 * node_cols] = mask
-
-    def note_copy(k):
-        offset = offsets[k]
-        return pltpu.make_async_remote_copy(
-            src_ref=notes.at[SPAN],
-            dst_ref=notes.at[SPAN - offset],
-            send_sem=note_send.at[k],
-            recv_sem=note_recv.at[SPAN - offset],
-            device_id={"row": me + offset},
-            device_id_type=pl.DeviceIdType.MESH,
-        )
+    notes[SPAN] = flow
 
     for k, offset in enumerate(offsets):
         @pl.when(inside(offset))
         def _():
-            note_copy(k).start()
-
+            row_copy(k, notes, note_send, note_recv).start()
+
+    for k, offset in enumerate(offsets):
+        @pl.when(inside(offset))
+        def _():
+            slot = SPAN + offset
+            pltpu.make_async_copy(
+                mask_notes.at[slot], mask_notes.at[slot], mask_recv.at[slot]
+            ).wait()
+            pltpu.make_async_copy(notes.at[slot], notes.at[slot], note_recv.at[slot]).wait()
+
+    rows_out[0] = notes[...]
+    rows_out[1] = mask_notes[...]
+
+    for side in range(2):
+        @on_side(side)
+        def _():
+            halo_copy(side).wait_send()
+            band_copy(side).wait_send()
+    for k, offset in enumerate(offsets):
+        @pl.when(inside(offset))
+        def _():
+            row_copy(k, mask_notes, mask_send, mask_recv).wait_send()
+            row_copy(k, notes, note_send, note_recv).wait_send()
+
+
+def relax_kernel(rows_of, rows, flows_out, moved_out):
+    me = lax.axis_index("row")
+    npairs, _, _, node_cols = flows_out.shape
+    count = moved_out.shape[0]
+    lane = lax.broadcasted_iota(jnp.int32, (8, LANES), 1)
+    line = lax.broadcasted_iota(jnp.int32, (8, LANES), 0)
+    flow = rows[0, SPAN]
     flows_out[:, 0, 0, :] = flow[:npairs, :node_cols]
     flows_out[:, 1, 0, :] = flow[:npairs, node_cols:]
-
-    for k, offset in enumerate(offsets):
-        @pl.when(inside(offset))
-        def _():
-            slot = SPAN + offset
-            pltpu.make_async_copy(notes.at[slot], notes.at[slot], note_recv.at[slot]).wait()
-
     node_row = me - SPAN + line
     keep = jnp.where((node_row >= 0) & (node_row < rows_of), 0.1, 0.0)
     at_left = (lane == 0) | (lane == node_cols)
     at_right = (lane == node_cols - 1) | (lane == 2 * node_cols - 1)
-    flow_rows = [notes[:, p, :] for p in range(npairs)]
-    mask_rows = [notes[:, 8 + p, :] for p in range(npairs)]
+    flow_rows = [rows[0, :, p, :] for p in range(npairs)]
+    mask_rows = [rows[1, :, p, :] for p in range(npairs)]
     moved = [jnp.zeros((8, LANES), F32) for _ in range(count)]
     for step in range(STEPS):
         grad = [None] * count
@@ -309,17 +351,6 @@
         moved_out[s, 0] = moved[s][SPAN:SPAN + 1, :node_cols]
         moved_out[s, 1] = moved[s][SPAN:SPAN + 1, node_cols:]
 
-    for side in range(2):
-        @on_side(side)
-        def _():
-            for s in range(1, count):
-                halo_copy(side, s).wait_send()
-            band_copy(side).wait_send()
-    for k, offset in enumerate(offsets):
-        @pl.when(inside(offset))
-        def _():
-            note_copy(k).wait_send()
-
 
 def local(rows_of, sections, valid):
     count, stride, width = sections.shape
@@ -328,43 +359,54 @@
     node_cols = width // stride
     moving = count - 1
     terms = TERMS * SHIFTS
-    return pl.pallas_call(
+    rows = pl.pallas_call(
         functools.partial(kernel, rows_of),
-        out_shape=(
-            jax.ShapeDtypeStruct((npairs, 2, 1, node_cols), F32),
-            jax.ShapeDtypeStruct((count, 2, 1, node_cols), F32),
-        ),
+        out_shape=jax.ShapeDtypeStruct((2, 8, 8, LANES), F32),
         in_specs=[
             pl.BlockSpec(memory_space=pl.ANY),
-            pl.BlockSpec(memory_space=pltpu.VMEM),
+            pl.BlockSpec(memory_space=pl.ANY),
         ],
-        out_specs=(
-            pl.BlockSpec(memory_space=pltpu.VMEM),
-            pl.BlockSpec(memory_space=pltpu.VMEM),
-        ),
+        out_specs=pl.BlockSpec(memory_space=pltpu.VMEM),
         scratch_shapes=[
             pltpu.VMEM((count, stride, width), F32),
-            pltpu.VMEM((count * stride * blocks, LANES), F32),
+            pltpu.VMEM((count, stride * blocks, LANES), F32),
             pltpu.VMEM((SHIFTS, moving, stride, blocks, LANES), F32),
             pltpu.VMEM((2, moving, RADIUS * blocks, LANES), F32),
             pltpu.VMEM((SHIFTS, 2, moving, RADIUS, blocks, LANES), F32),
             pltpu.VMEM((2, blocks // 8, -(-terms // 8) * 64, LANES), F32),
             pltpu.VMEM((width, LANES), BF16),
-            pltpu.VMEM((2, LANES, LANES), F32),
-            pltpu.VMEM((2, LANES, LANES), F32),
-            pltpu.VMEM((8, 16, LANES), F32),
+            pltpu.VMEM((2, LANES // 2, LANES), F32),
+            pltpu.VMEM((2, LANES // 2, LANES), F32),
+            pltpu.VMEM((8, 8, LANES), F32),
             pltpu.SemaphoreType.DMA((count,)),
-            pltpu.SemaphoreType.DMA((2, moving)),
-            pltpu.SemaphoreType.DMA((2, moving)),
+            pltpu.SemaphoreType.DMA((2,)),
+            pltpu.SemaphoreType.DMA((2,)),
             pltpu.SemaphoreType.DMA((2,)),
             pltpu.SemaphoreType.DMA((2,)),
             pltpu.SemaphoreType.DMA((2 * SPAN,)),
             pltpu.SemaphoreType.DMA((2 * SPAN + 1,)),
+            pltpu.VMEM(valid.shape, jnp.int32),
+            pltpu.VMEM((8, 8, LANES), F32),
+            pltpu.SemaphoreType.DMA,
+            pltpu.SemaphoreType.DMA((2 * SPAN,)),
+            pltpu.SemaphoreType.DMA((2 * SPAN + 1,)),
         ],
         compiler_params=pltpu.CompilerParams(
-            collective_id=0, has_side_effects=True, vmem_limit_bytes=32 * 2**20
+            collective_id=0, has_side_effects=True, vmem_limit_bytes=60 * 2**20
         ),
     )(sections, valid)
+    return pl.pallas_call(
+        functools.partial(relax_kernel, rows_of),
+        out_shape=(
+            jax.ShapeDtypeStruct((npairs, 2, 1, node_cols), F32),
+            jax.ShapeDtypeStruct((count, 2, 1, node_cols), F32),
+        ),
+        in_specs=[pl.BlockSpec(memory_space=pltpu.VMEM)],
+        out_specs=(
+            pl.BlockSpec(memory_space=pltpu.VMEM),
+            pl.BlockSpec(memory_space=pltpu.VMEM),
+        ),
+    )(rows)
 
 
 def solution(mesh):

time: 20.7 us -> 17.9 us (0.86)
  local copies, waits for them, and re-layouts: 3.09 us -> 0 us
  Pallas kernels: 16.8 us -> 17.1 us
    unnamed x6 -> x0, local copies, waits for them, and re-layouts: 3.09 us -> none
    pallas_call x1 -> x2, Pallas kernels: 16.8 us -> 17.1 us  [the longest x1 15.3 us: local(): pl.pallas_call(functools.partial(kernel, rows_of), out_shape=jax.ShapeDty...]
where the time goes in v2:
time: 17.9 us; the launch traced here: 17.7 us
  Pallas kernels  17.1 us (96%)
  between operations  0.64 us (4%)
    pallas_call x1, Pallas kernels, local(): pl.pallas_call(functools.partial(kernel, rows_of), out_shape=jax.ShapeDty...  15.3 us
    pallas_call x1, Pallas kernels, local(): pl.pallas_call(functools.partial(relax_kernel, rows_of), out_shape=(jax.S...  1.81 us

profile of v2, /device:TPU:1, one launch (start us, length us, event | category | flops | bytes accessed | tf_op | source)
XLA Modules:
  0.0 17.7 jit_solution(8798406539447560635)
XLA Ops:
  0.6 15.3 %shard_map.41.rows = f32[2,8,8,128]{3,2,1,0:T(8,128)} custom-call(f32[4,32,2048]{2,1,0:T(8,128)} %sections.1, s32[5,1,64]{2,1,0:T(1,128)} %valid.1), custom_call_target="tpu_custom_call" | custom-call | tf_op jit(solution)/shard_map/pallas_call | solution.py:362
  15.9 1.8 %shard_map.42 = (f32[5,2,1,64]{3,2,1,0:T(1,128)}, f32[4,2,1,64]{3,2,1,0:T(1,128)}) custom-call(f32[2,8,8,128]{3,2,1,0:T(8,128)} %shard_map.41.rows), custom_call_target="tpu_custom_call" | custom-call | tf_op jit(solution)/shard_map/pallas_call | solution.py:398

commit v3 on v2

--- a/solution.py
+++ b/solution.py
@@ -25,14 +25,6 @@
     middle = rest.astype(BF16)
     low = (rest - middle.astype(F32)).astype(BF16)
     return high, middle, low
-
-
-def exact_dot(value, ones):
-    rows = value.shape[0]
-    parts = jnp.dot(
-        jnp.concatenate(thirds(value), axis=0), ones, preferred_element_type=F32
-    )
-    return parts[:rows] + parts[rows:2 * rows] + parts[2 * rows:]
 
 
 def shifted(row, shift):
@@ -75,7 +67,7 @@
     notes[...] = jnp.zeros(notes.shape, F32)
     mask_notes[...] = jnp.zeros(mask_notes.shape, F32)
     barrier = pltpu.get_barrier_semaphore()
-    offsets = [o for k in range(1, SPAN + 1) for o in (-k, k)]
+    offsets = [o for k in range(SPAN, 0, -1) for o in (-k, k)]
 
     def inside(offset):
         return me >= -offset if offset < 0 else me < rows_of - offset
@@ -104,7 +96,7 @@
     for s in range(count):
         loads[s].wait()
 
-        @pl.loop(0, stride // 8)
+        @pl.loop(0, stride // 8, unroll=4)
         def _(tile):
             base = pl.multiple_of(tile * 8 * blocks, 8)
             top = pl.multiple_of(tile * 8, 8)
@@ -159,7 +151,7 @@
         def _():
             row_copy(k, mask_notes, mask_send, mask_recv).start()
 
-    @pl.loop(0, stride, unroll=8)
+    @pl.loop(0, stride, unroll=16)
     def _(row):
         for s in range(1, count):
             start = pl.multiple_of(row * blocks, 8)
@@ -205,7 +197,7 @@
                 for x in range(SHIFTS):
                     halo_moving[x, side, s, row] = shifted(value, x - RADIUS)
 
-    @pl.loop(0, SHIFTS * halves)
+    @pl.loop(0, SHIFTS * halves, unroll=5)
     def _(turn):
         x = turn // halves
         half = turn % halves
@@ -241,14 +233,27 @@
         )
 
     first_half = lax.broadcasted_iota(jnp.int32, (LANES // 2, LANES), 1) < node_cols
+    total = jnp.zeros((6 * LANES, LANES), F32)
+    for t in range(0, blocks, 2):
+        wide = jnp.concatenate(
+            [
+                jnp.concatenate(
+                    [sums[b, k // 8, pl.ds(k % 8, LANES, stride=8), :] for k in (t, t + 1)],
+                    axis=1,
+                )
+                for b in range(2)
+            ],
+            axis=0,
+        )
+        total = total + jnp.dot(
+            jnp.concatenate(thirds(wide), axis=0),
+            ones[t * LANES:(t + 2) * LANES, :],
+            preferred_element_type=F32,
+        )
+    total = total[:2 * LANES] + total[2 * LANES:4 * LANES] + total[4 * LANES:]
     for b in range(2):
-        total = jnp.zeros((LANES, LANES), F32)
-        for t in range(0, blocks, 2):
-            wide = jnp.concatenate(
-                [sums[b, k // 8, pl.ds(k % 8, LANES, stride=8), :] for k in (t, t + 1)], axis=1
-            )
-            total = total + exact_dot(wide, ones[t * LANES:(t + 2) * LANES, :])
-        reduced[b] = jnp.where(first_half, total[:LANES // 2], total[LANES // 2:])
+        part = total[b * LANES:(b + 1) * LANES]
+        reduced[b] = jnp.where(first_half, part[:LANES // 2], part[LANES // 2:])
 
         @on_side(b)
         def _():

time: 17.9 us -> 17.1 us (0.955)
  the two profiles are of different devices: /device:TPU:1 before, /device:TPU:0 now
where the time goes in v3:
time: 17.1 us; the launch traced here: 16.9 us
  Pallas kernels  16.2 us (95%)
  between operations  0.64 us (4%)
    pallas_call x1, Pallas kernels, local(): pl.pallas_call(functools.partial(kernel, rows_of), out_shape=jax.ShapeDty...  14.4 us
    pallas_call x1, Pallas kernels, local(): pl.pallas_call(functools.partial(relax_kernel, rows_of), out_shape=(jax.S...  1.81 us

profile of v3, /device:TPU:0, one launch (start us, length us, event | category | flops | bytes accessed | tf_op | source)
XLA Modules:
  0.0 16.9 jit_solution(3101022311877666860)
XLA Ops:
  0.6 14.4 %shard_map.41.rows = f32[2,8,8,128]{3,2,1,0:T(8,128)} custom-call(f32[4,32,2048]{2,1,0:T(8,128)} %sections.1, s32[5,1,64]{2,1,0:T(1,128)} %valid.1), custom_call_target="tpu_custom_call" | custom-call | tf_op jit(solution)/shard_map/pallas_call | solution.py:367
  15.1 1.8 %shard_map.42 = (f32[5,2,1,64]{3,2,1,0:T(1,128)}, f32[4,2,1,64]{3,2,1,0:T(1,128)}) custom-call(f32[2,8,8,128]{3,2,1,0:T(8,128)} %shard_map.41.rows), custom_call_target="tpu_custom_call" | custom-call | tf_op jit(solution)/shard_map/pallas_call | solution.py:403

commit v4 on v3

--- a/solution.py
+++ b/solution.py
@@ -105,6 +105,14 @@
                     s, pl.ds(top, 8), t * LANES:(t + 1) * LANES
                 ]
 
+    @pl.loop(0, stride // 2, unroll=16)
+    def _(row):
+        for s in range(1, count):
+            start = pl.multiple_of(row * blocks, 8)
+            value = image[s, pl.ds(start, blocks), :]
+            for x in range(SHIFTS):
+                moving[x, s - 1, row] = shifted(value, x - RADIUS)
+
     size = RADIUS * blocks
     signals = jnp.minimum(me, SPAN) + jnp.minimum(rows_of - 1 - me, SPAN)
     pl.semaphore_wait(barrier, signals)
@@ -142,16 +150,7 @@
             device_id_type=pl.DeviceIdType.MESH,
         )
 
-    mask_copy_in.wait()
-    mask = mask_in[:, 0, :].astype(F32)
-    mask_notes[SPAN, 0:npairs, 0:node_cols] = mask
-    mask_notes[SPAN, 0:npairs, node_cols:2 * node_cols] = mask
-    for k, offset in enumerate(offsets):
-        @pl.when(inside(offset))
-        def _():
-            row_copy(k, mask_notes, mask_send, mask_recv).start()
-
-    @pl.loop(0, stride, unroll=16)
+    @pl.loop(stride // 2, stride, unroll=16)
     def _(row):
         for s in range(1, count):
             start = pl.multiple_of(row * blocks, 8)
@@ -183,6 +182,15 @@
                         totals[i] = product if totals[i] is None else totals[i] + product
             for i in range(TERMS):
                 sums[b, half, pl.ds(pl.multiple_of(out + i * 8, 8), 8), :] = totals[i]
+
+    mask_copy_in.wait()
+    mask = mask_in[:, 0, :].astype(F32)
+    mask_notes[SPAN, 0:npairs, 0:node_cols] = mask
+    mask_notes[SPAN, 0:npairs, node_cols:2 * node_cols] = mask
+    for k, offset in enumerate(offsets):
+        @pl.when(inside(offset))
+        def _():
+            row_copy(k, mask_notes, mask_send, mask_recv).start()
 
     for side in range(2):
         @on_side(side)

time: 17.1 us -> 17 us (level)
  the two profiles are of different devices: /device:TPU:0 before, /device:TPU:1 now
where the time goes in v4:
time: 17 us; the launch traced here: 16.8 us
  Pallas kernels  16.2 us (95%)
  between operations  0.64 us (4%)
    pallas_call x1, Pallas kernels, local(): pl.pallas_call(functools.partial(kernel, rows_of), out_shape=jax.ShapeDty...  14.4 us
    pallas_call x1, Pallas kernels, local(): pl.pallas_call(functools.partial(relax_kernel, rows_of), out_shape=(jax.S...  1.81 us

profile of v4, /device:TPU:1, one launch (start us, length us, event | category | flops | bytes accessed | tf_op | source)
XLA Modules:
  0.0 16.8 jit_solution(2102816232421533840)
XLA Ops:
  0.6 14.4 %shard_map.41.rows = f32[2,8,8,128]{3,2,1,0:T(8,128)} custom-call(f32[4,32,2048]{2,1,0:T(8,128)} %sections.1, s32[5,1,64]{2,1,0:T(1,128)} %valid.1), custom_call_target="tpu_custom_call" | custom-call | tf_op jit(solution)/shard_map/pallas_call | solution.py:375
  15.0 1.8 %shard_map.42 = (f32[5,2,1,64]{3,2,1,0:T(1,128)}, f32[4,2,1,64]{3,2,1,0:T(1,128)}) custom-call(f32[2,8,8,128]{3,2,1,0:T(8,128)} %shard_map.41.rows), custom_call_target="tpu_custom_call" | custom-call | tf_op jit(solution)/shard_map/pallas_call | solution.py:411
